TPU v7x, 128 devices: a whole 4x4x4 slice. The times are simulated.
128 devices in a mesh: tile: 16 (over z, y), seq: 8 (over x, core).
Axes of the slice: x: 4, y: 4, z: 4, core: 2. Of those that a mesh axis runs over, the one named last changes fastest.
Arguments:
- cls_tokens: bfloat16 [16384, 1536], P(('tile', 'seq')), may hold values from -6 to 6
- norm_gain: float32 [1536], replicated, may hold values from 0.5 to 1.5
- w_gate: bfloat16 [1536, 4096], P(None, 'tile'), may hold values from -0.15625 to 0.15625
- w_up: bfloat16 [1536, 4096], P(None, 'tile'), may hold values from -0.15625 to 0.15625
- w_down: bfloat16 [4096, 1536], P('tile'), may hold values from -0.09375 to 0.09375
- layer_scale: float32 [1536], replicated, may hold values from 0.25 to 1.75
- final_gain: float32 [1536], replicated, may hold values from 0.5 to 1.5
- w_embed: bfloat16 [1536, 768], replicated, may hold values from -0.15625 to 0.15625
- dest_pos: int32 [16384], P(('tile', 'seq')), may hold values from 0 to 16383, as said below
- tile_coords: int32 [2, 16384], P(None, ('tile', 'seq')), may hold values from 0 to 999
- attn_gain: float32 [768], replicated, may hold values from 0.5 to 1.5
- w_qkv: bfloat16 [768, 2304], replicated, may hold values from -4 to 4
- offsets: int32 [12], replicated, may hold values from 0 to 15
- w_out: bfloat16 [768, 768], replicated, may hold values from -0.21875 to 0.21875
Outputs:
- slide_out: bfloat16 [16384, 768], P(('tile', 'seq'))
Inputs may be any that keep to these rules, and one draw needn't show every extreme that they name: dest_pos holds each number of 0 to 16383 once; the 128 rows of one device go to the devices of the slide order in groups of 0, 1 or 2 rows a device, some pair carrying 2; every device receives 128 rows, 2 of them from the device 128 / 2 places before it in the slide order, counted round.
All inputs are finite; a program needn't handle non-finite values.
Results may differ from a plain program's by a relative error of at most 0.018.
Values may be sent and summed in bfloat16 or wider, within the bound.
No kernel may reach another device: no remote copies, remote signals or barrier semaphores. Data moves between devices by JAX's collectives and lax.ppermute only.
A program may use at most 128 MiB of HBM per device.

v0:
```python
import jax
import jax.numpy as jnp
from jax import lax
from jax.sharding import PartitionSpec as P

HEAD_COUNT = 12
HEAD_WIDTH = 64
SEGMENT_SPACING = 16


def layer_norm(sender_rows, gain):
    average = jnp.mean(sender_rows, axis=-1, keepdims=True)
    centered = sender_rows - average
    variance = jnp.mean(centered * centered, axis=-1, keepdims=True)
    return centered * lax.rsqrt(variance + 1e-06) * gain


def position_table(coords, hidden_width):
    quarter = hidden_width // 4
    frequency = 1.0 / 10000.0 ** (jnp.arange(quarter).astype(jnp.float32) / quarter)
    along_x = coords[:, 0:1].astype(jnp.float32) * frequency[None, :]
    along_y = coords[:, 1:2].astype(jnp.float32) * frequency[None, :]
    return jnp.concatenate(
        [jnp.sin(along_x), jnp.cos(along_x), jnp.sin(along_y), jnp.cos(along_y)], axis=1
    )


def attend(queries, key_rows, values):
    score_scale = queries.shape[-1] ** (-0.5)
    scores = (
        jnp.einsum("qhd,khd->hqk", queries, key_rows, preferred_element_type=jnp.float32)
        * score_scale
    )
    highest = jnp.max(scores, axis=-1, keepdims=True)
    weights = jnp.exp(scores - highest)
    totals = jnp.sum(weights, axis=-1, keepdims=True)
    mixed_rows = jnp.einsum(
        "hqk,khd->qhd", weights.astype(jnp.bfloat16), values, preferred_element_type=jnp.float32
    )
    result = mixed_rows / jnp.transpose(totals, (1, 0, 2))
    logsum = jnp.transpose((highest + jnp.log(totals))[:, :, 0])
    return (result, logsum)


def body(
    cls_tokens,
    norm_gain,
    w_gate,
    w_up,
    w_down,
    layer_scale,
    final_gain,
    w_embed,
    dest_pos,
    tile_coords,
    attn_gain,
    w_qkv,
    offsets,
    w_out,
):
    resident_rows = cls_tokens.shape[0]
    tokens = cls_tokens.astype(jnp.float32)
    normed = layer_norm(tokens, norm_gain).astype(jnp.bfloat16)
    shard_rows = lax.all_gather(normed, "tile", axis=0, tiled=True)
    gate_proj = jnp.dot(shard_rows, w_gate, preferred_element_type=jnp.float32)
    upward = jnp.dot(shard_rows, w_up, preferred_element_type=jnp.float32)
    hidden = (jax.nn.silu(gate_proj) * upward).astype(jnp.bfloat16)
    projected = lax.psum_scatter(
        jnp.dot(hidden, w_down, preferred_element_type=jnp.float32),
        "tile",
        scatter_dimension=0,
        tiled=True,
    )
    mixed_rows = tokens + layer_scale * projected
    final_rows = layer_norm(mixed_rows, final_gain).astype(jnp.bfloat16)
    embedded = jnp.dot(final_rows, w_embed, preferred_element_type=jnp.float32).astype(jnp.bfloat16)
    hidden_width = embedded.shape[1]
    tile_count = lax.axis_size("tile")
    seq_count = lax.axis_size("seq")
    devices = tile_count * seq_count
    capacity = 2 * max(1, resident_rows // devices)
    target = dest_pos // resident_rows
    row_ids = jnp.arange(resident_rows)
    earlier = (target[:, None] == target[None, :]) & (row_ids[None, :] < row_ids[:, None])
    slot_index = jnp.sum(earlier.astype(jnp.int32), axis=1)
    where_to = target * capacity + slot_index
    payload = jnp.zeros((devices * capacity, hidden_width), jnp.bfloat16).at[where_to].set(embedded)
    meta_rows = jnp.stack([dest_pos, tile_coords[0], tile_coords[1]], axis=1)
    meta_table = jnp.full((devices * capacity, 3), -1, jnp.int32).at[where_to].set(meta_rows)
    received, received_meta = (
        lax.all_to_all(
            payload.reshape(devices, capacity, hidden_width),
            ("tile", "seq"),
            split_axis=0,
            concat_axis=0,
            tiled=True,
        ),
        lax.all_to_all(
            meta_table.reshape(devices, capacity, 3),
            ("tile", "seq"),
            split_axis=0,
            concat_axis=0,
            tiled=True,
        ),
    )
    flat_rows = received.reshape(-1, hidden_width)
    flat_meta = received_meta.reshape(-1, 3)
    is_live = flat_meta[:, 0] >= 0
    local_slot = jnp.where(is_live, flat_meta[:, 0] % resident_rows, resident_rows)
    placed = (
        jnp.zeros((resident_rows, hidden_width), jnp.bfloat16)
        .at[local_slot]
        .set(flat_rows, mode="drop")
    )
    coords = (
        jnp.zeros((resident_rows, 2), jnp.int32).at[local_slot].set(flat_meta[:, 1:], mode="drop")
    )
    seq_in = placed.astype(jnp.float32) + position_table(coords, hidden_width)
    normed_seq = layer_norm(seq_in, attn_gain).astype(jnp.bfloat16)
    qkv = jnp.dot(normed_seq, w_qkv, preferred_element_type=jnp.float32).astype(jnp.bfloat16)
    queries = qkv[:, :hidden_width]
    keys_values = qkv[:, hidden_width:]
    segment_kv = lax.all_gather(keys_values, "seq", axis=0, tiled=True)
    near_out, nearby_logsumexp = attend(
        queries.reshape(resident_rows, HEAD_COUNT, HEAD_WIDTH),
        segment_kv[:, :hidden_width].reshape(-1, HEAD_COUNT, HEAD_WIDTH),
        segment_kv[:, hidden_width:].reshape(-1, HEAD_COUNT, HEAD_WIDTH),
    )
    kept_rows = jnp.arange(SEGMENT_SPACING, dtype=jnp.int32)[:, None] == offsets[None, :]

    def select(sender_rows, stacked_rows):
        head_grouped = sender_rows.reshape(
            resident_rows // SEGMENT_SPACING, SEGMENT_SPACING, stacked_rows, HEAD_COUNT, HEAD_WIDTH
        )
        sampled_rows = jnp.sum(
            jnp.where(
                kept_rows[None, :, None, :, None], head_grouped, jnp.zeros((), sender_rows.dtype)
            ),
            axis=1,
        )
        return sampled_rows.reshape(resident_rows // SEGMENT_SPACING, stacked_rows * hidden_width)

    far_kv = lax.all_gather(select(keys_values, 2), ("tile", "seq"), axis=0, tiled=True)
    far_out, far_lse = attend(
        select(queries, 1).reshape(-1, HEAD_COUNT, HEAD_WIDTH),
        far_kv[:, :hidden_width].reshape(-1, HEAD_COUNT, HEAD_WIDTH),
        far_kv[:, hidden_width:].reshape(-1, HEAD_COUNT, HEAD_WIDTH),
    )
    far_full = jnp.where(kept_rows[None, :, :, None], far_out[:, None], 0.0).reshape(
        resident_rows, HEAD_COUNT, HEAD_WIDTH
    )
    nearby_grouped = nearby_logsumexp.reshape(
        resident_rows // SEGMENT_SPACING, SEGMENT_SPACING, HEAD_COUNT
    )
    far_share = jnp.where(
        kept_rows[None], 1.0 / (1.0 + jnp.exp(nearby_grouped - far_lse[:, None])), 0.0
    ).reshape(resident_rows, HEAD_COUNT)
    combined = (1.0 - far_share)[:, :, None] * near_out + far_share[:, :, None] * far_full
    attn_rows = combined.reshape(resident_rows, hidden_width).astype(jnp.bfloat16)
    return (seq_in + jnp.dot(attn_rows, w_out, preferred_element_type=jnp.float32)).astype(
        jnp.bfloat16
    )


def solution(mesh):
    in_specs = (
        P(("tile", "seq"), None),
        P(),
        P(None, "tile"),
        P(None, "tile"),
        P("tile", None),
        P(),
        P(),
        P(),
        P(("tile", "seq")),
        P(None, ("tile", "seq")),
        P(),
        P(),
        P(),
        P(),
    )
    out_specs = P(("tile", "seq"), None)
    return jax.shard_map(body, mesh=mesh, in_specs=in_specs, out_specs=out_specs, check_vma=False)
```

profile of v0, /device:TPU:1, one launch (start us, length us, event | category | flops | bytes accessed | tf_op | source)
XLA Modules:
  0.0 357.2 jit_solution(11485548192163310712)
XLA Ops:
  9.1 2.0 fusion.33
  11.2 64.7 %all-gather.4.cloned.1.call-done = bf16[2048,1536]{1,0:T(8,128)(2,1)} async-done(((bf16[128,1536]{1,0:T(8,128)(2,1)}), bf16[2048,1536]{1,0:T(8,128)(2,1)}) %all-gather.4.cloned.1.call-update) | async-done | bytes 6291472 | tf_op jit(solution)/shard_map/all_gather | solution.py:64
  75.9 6.1 %fusion.70 = f32[2048,256]{1,0:T(8,128)} fusion(bf16[2048,1536]{1,0:T(8,128)(2,1)} %all-gather.4.cloned.1.call-done, bf16[1536,256]{1,0:T(8,128)(2,1)} %param.16), kind=kOutput, calls=%fused_computation.112 | convolution fusion | flops 1610612736 | bytes 9175040 | tf_op jit(solution)/shard_map/dot_general | solution.py:65
  82.0 14.6 %fusion.7 = f32[2048,1536]{1,0:T(8,128)} fusion(bf16[256,1536]{1,0:T(8,128)(2,1)} %param.18, bf16[2048,1536]{1,0:T(8,128)(2,1)} %all-gather.4.cloned.1.call-done, bf16[1536,256]{1,0:T(8,128)(2,1)} %param.17, f32[2048,256]{1,0:T(8,128)} %fusion.70), kind=kOutput, calls=%fused_computation.14 | convolution fusion | flops 3224371200 | bytes 22544384 | tf_op jit(solution)/shard_map/dot_general | solution.py:69
  103.8 8.3 %all-to-all-start = ((s32[128,2,3]{2,1,0:T(2,128)}), s32[128,2,3]{2,1,0:T(2,128)}, u32[]{:S(2)}, u32[]{:S(2)}) async-start(s32[128,2,3]{2,1,0:T(2,128)} %bitcast.76), calls=%async_computation | async-start | bytes 262144 | tf_op jit(solution)/shard_map/all_to_all | solution.py:98
  112.8 9.2 %all-to-all-done = s32[128,2,3]{2,1,0:T(2,128)} async-done(((s32[128,2,3]{2,1,0:T(2,128)}), s32[128,2,3]{2,1,0:T(2,128)}, u32[]{:S(2)}, u32[]{:S(2)}) %all-to-all-start) | async-done | bytes 3104 | tf_op jit(solution)/shard_map/all_to_all | solution.py:98
  123.5 68.9 %reduce-scatter.2.cloned.1.call-done = f32[128,1536]{1,0:T(8,128)} async-done(((f32[2048,1536]{1,0:T(8,128)}), f32[128,1536]{1,0:T(8,128)}) %reduce-scatter.2.cloned.1.call-update) | async-done | bytes 786448 | tf_op jit(solution)/shard_map/reduce_scatter | solution.py:68
  195.4 2.9 convolution_convert_fusion.1
  198.3 2.3 scatter_custom_fusion.1
  200.6 1.9 reshape.194
  202.5 7.8 %all-to-all-start.1 = ((bf16[128,2,768]{2,1,0:T(2,128)(2,1)}), bf16[128,2,768]{2,1,0:T(2,128)(2,1)}, u32[]{:S(2)}, u32[]{:S(2)}) async-start(bf16[128,2,768]{2,1,0:T(2,128)(2,1)} %reshape.194), calls=%async_computation.2 | async-start | bytes 786432 | tf_op jit(solution)/shard_map/all_to_all | solution.py:91
  211.0 2.2 scatter_custom_fusion.3
  214.3 2.5 multiply_sine_fusion.1
  216.7 5.6 %all-to-all-done.1 = bf16[128,2,768]{2,1,0:T(2,128)(2,1)} async-done(((bf16[128,2,768]{2,1,0:T(2,128)(2,1)}), bf16[128,2,768]{2,1,0:T(2,128)(2,1)}, u32[]{:S(2)}, u32[]{:S(2)}) %all-to-all-start.1) | async-done | bytes 393248 | tf_op jit(solution)/shard_map/all_to_all | solution.py:91
  222.3 1.9 reshape.224
  224.2 2.7 scatter_custom_fusion.2
  231.0 2.6 reshape.199
  233.5 2.2 select_reduce_fusion
  242.8 2.1 reshape.198
  246.8 8.7 %all-gather.6.cloned.1.call-done = bf16[1024,1536]{1,0:T(8,128)(2,1)} async-done(((bf16[128,1536]{1,0:T(8,128)(2,1)}), bf16[1024,1536]{1,0:T(8,128)(2,1)}) %all-gather.6.cloned.1.call-update) | async-done | bytes 3145744 | tf_op jit(solution)/shard_map/all_gather | solution.py:123
  255.4 3.8 %fusion.68 = (bf16[1024,768]{1,0:T(8,128)(2,1)}, bf16[1024,768]{1,0:T(8,128)(2,1)}) fusion(bf16[1024,1536]{1,0:T(8,128)(2,1)} %all-gather.6.cloned.1.call-done), kind=kLoop, calls=%fused_computation.110 | loop fusion | bytes 6291456 | tf_op jit(solution)/shard_map/slice | solution.py:126
  259.2 2.6 copy.82
  261.9 2.6 copy.85
  264.5 2.6 multiply_reduce_fusion
  267.1 2.7 copy-done.1
  271.7 52.7 %all-gather.8.cloned.1.call-done = bf16[1024,1536]{1,0:T(8,128)(2,1)} async-done(((bf16[8,1536]{1,0:T(8,128)(2,1)}), bf16[1024,1536]{1,0:T(8,128)(2,1)}) %all-gather.8.cloned.1.call-update) | async-done | bytes 3145744 | tf_op jit(solution)/shard_map/all_gather | solution.py:143
  324.3 3.8 %fusion.67 = (bf16[1024,768]{1,0:T(8,128)(2,1)}, bf16[1024,768]{1,0:T(8,128)(2,1)}) fusion(bf16[1024,1536]{1,0:T(8,128)(2,1)} %all-gather.8.cloned.1.call-done), kind=kLoop, calls=%fused_computation.109 | loop fusion | bytes 6291456 | tf_op jit(solution)/shard_map/slice | solution.py:146
  328.1 2.6 copy.83
  336.2 2.6 copy.86
  338.8 2.1 fusion.15
  341.9 2.1 copy.89
  344.8 4.8 %fusion.26 = bf16[128,12,64]{0,2,1:T(8,128)(2,1)S(1)} fusion(bf16[1024,12,64]{0,2,1:T(8,128)(2,1)} %bitcast.74, f32[12,128,1024]{2,1,0:T(8,128)} %copy-done.1, f32[12,128]{1,0:T(8,128)S(1)} %get-tuple-element.23, f32[128,12,64]{0,2,1:T(8,128)} %copy.89, f32[128,12]{0,1:T(8,128)S(1)} %get-tuple-element.8, f32[128,12]{0,1:T(8,128)} %bitcast.79, ...), kind=kOutput, calls=%fused_computation.33 | convolution fusion | flops 206635008 | bytes 8480256 | tf_op jit(solution)/shard_map/hqk,khd->qhd/dot_general | solution.py:37
  (77 shorter events, 39.8 us)
Async XLA Ops:
  6.5 222.0 %copy-start = (bf16[768,2304]{1,0:T(8,128)(2,1)S(1)}, bf16[768,2304]{1,0:T(8,128)(2,1)}, u32[]{:S(2)}) copy-start(bf16[768,2304]{1,0:T(8,128)(2,1)} %param.25) | copy-start | bytes 10616836
  6.5 69.4 %all-gather.4.cloned.1.call-start = ((), (), s32[]{:S(2)}) async-start(), calls=%async_computation.3 | async-start | bytes 6684672 | tf_op jit(solution)/shard_map/all_gather | solution.py:64
  11.1 181.2 %reduce-scatter.2.cloned.1.call-start = ((), (), s32[]{:S(2)}) async-start(), calls=%async_computation.4 | async-start | bytes 13369344 | tf_op jit(solution)/shard_map/reduce_scatter | solution.py:68
  96.6 95.8 %copy-start.9 = (f32[1536]{0:T(1024)S(1)}, f32[1536]{0:T(1024)}, u32[]{:S(2)}) copy-start(f32[1536]{0:T(1024)} %param.19) | copy-start | bytes 18436
  96.6 98.8 %copy-start.11 = (f32[1536]{0:T(1024)S(1)}, f32[1536]{0:T(1024)}, u32[]{:S(2)}) copy-start(f32[1536]{0:T(1024)} %param.20) | copy-start | bytes 18436
  103.8 18.1 %all-to-all-start = ((s32[128,2,3]{2,1,0:T(2,128)}), s32[128,2,3]{2,1,0:T(2,128)}, u32[]{:S(2)}, u32[]{:S(2)}) async-start(s32[128,2,3]{2,1,0:T(2,128)} %bitcast.76), calls=%async_computation | async-start | bytes 262144 | tf_op jit(solution)/shard_map/all_to_all | solution.py:98
  192.4 3.0 copy-start.2
  192.4 3.0 copy-start.3
  200.6 28.0 %copy-start.12 = (f32[768]{0:T(1024)S(1)}, f32[768]{0:T(1024)}, u32[]{:S(2)}) copy-start(f32[768]{0:T(1024)} %param.24) | copy-start | bytes 9220
  202.5 19.8 %all-to-all-start.1 = ((bf16[128,2,768]{2,1,0:T(2,128)(2,1)}), bf16[128,2,768]{2,1,0:T(2,128)(2,1)}, u32[]{:S(2)}, u32[]{:S(2)}) async-start(bf16[128,2,768]{2,1,0:T(2,128)(2,1)} %reshape.194), calls=%async_computation.2 | async-start | bytes 786432 | tf_op jit(solution)/shard_map/all_to_all | solution.py:91
  210.3 45.2 %all-gather.6.cloned.1.call-start = ((), (), s32[]{:S(2)}) async-start(), calls=%async_computation.5 | async-start | bytes 3538944 | tf_op jit(solution)/shard_map/all_gather | solution.py:123
  228.3 0.9 copy-start.4
  228.5 2.4 copy-start.13
  229.2 0.8 copy-start.7
  230.9 93.4 %all-gather.8.cloned.1.call-start = ((), (), s32[]{:S(2)}) async-start(), calls=%async_computation.6 | async-start | bytes 3170304 | tf_op jit(solution)/shard_map/all_gather | solution.py:143
  267.1 2.7 copy-start.1
  332.5 0.7 copy-start.6
  333.5 0.6 copy-start.10
  344.8 4.8 %copy-start.5 = (f32[128,768]{1,0:T(8,128)S(1)}, f32[128,768]{1,0:T(8,128)}, u32[]{:S(2)}) copy-start(f32[128,768]{1,0:T(8,128)} %copy-done.4) | copy-start | bytes 1179652
  344.8 4.8 %copy-start.8 = (bf16[768,768]{1,0:T(8,128)(2,1)S(1)}, bf16[768,768]{1,0:T(8,128)(2,1)}, u32[]{:S(2)}) copy-start(bf16[768,768]{1,0:T(8,128)(2,1)} %param.27) | copy-start | bytes 3538948
Sparse Core Ops, SparseCore 0:
  11.3 64.6 all-gather.3
  96.7 95.5 reduce-scatter.1
  231.0 24.3 all-gather.5
  258.4 65.8 all-gather.7
where the time goes:
time: 358 us; the launch traced here: 357 us
  waiting for transfers between devices  210 us (59%)
  local copies, waits for them, and re-layouts  56.9 us (16%)
  matrix products  36.7 us (10%)
  other arithmetic  24.2 us (7%)
  starting transfers between devices  16.2 us (5%)
  between operations  13.4 us (4%)
    reduce_scatter x1, waiting for transfers between devices, body(): lax.psum_scatter(jnp.dot(hidden, w_down, preferred_element_type=jnp.float...  68.9 us
    all_gather x1, waiting for transfers between devices, body(): shard_rows = lax.all_gather(normed, 'tile', axis=0, tiled=True)  64.7 us
    all_gather x1, waiting for transfers between devices, body(): lax.all_gather(select(keys_values, 2), ('tile', 'seq'), axis=0, tiled=True)  52.7 us
    dot_general x1, matrix products, body(): jnp.dot(hidden, w_down, preferred_element_type=jnp.float32)  14.6 us
    all_to_all x1, waiting for transfers between devices, body(): lax.all_to_all(meta_table.reshape(devices, capacity, 3), ('tile', 'seq'),...  9.2 us
    all_gather x1, waiting for transfers between devices, body(): segment_kv = lax.all_gather(keys_values, 'seq', axis=0, tiled=True)  8.69 us
    all_to_all x1, starting transfers between devices, body(): lax.all_to_all(meta_table.reshape(devices, capacity, 3), ('tile', 'seq'),...  8.32 us
    all_to_all x1, starting transfers between devices, body(): lax.all_to_all(payload.reshape(devices, capacity, hidden_width), ('tile',...  7.79 us
  transfers between devices with their start and end apart: 6, of which 6 were waited for; matrix products, arithmetic and copies ran while one was open for 13% of the time, Pallas kernels for 0%

commit v1 on v0

--- a/solution.py
+++ b/solution.py
@@ -6,6 +6,11 @@
 HEAD_COUNT = 12
 HEAD_WIDTH = 64
 SEGMENT_SPACING = 16
+
+
+def gather_by_exchange(x, axis, dim):
+    copies = jnp.concatenate([x] * lax.axis_size(axis), axis=dim)
+    return lax.all_to_all(copies, axis, dim, dim, tiled=True)
 
 
 def layer_norm(sender_rows, gain):
@@ -120,7 +125,7 @@
     qkv = jnp.dot(normed_seq, w_qkv, preferred_element_type=jnp.float32).astype(jnp.bfloat16)
     queries = qkv[:, :hidden_width]
     keys_values = qkv[:, hidden_width:]
-    segment_kv = lax.all_gather(keys_values, "seq", axis=0, tiled=True)
+    segment_kv = gather_by_exchange(keys_values, "seq", 0)
     near_out, nearby_logsumexp = attend(
         queries.reshape(resident_rows, HEAD_COUNT, HEAD_WIDTH),
         segment_kv[:, :hidden_width].reshape(-1, HEAD_COUNT, HEAD_WIDTH),

time: 358 us -> 323 us (0.902)
  local copies, waits for them, and re-layouts: 56.9 us -> 38.8 us
  waiting for transfers between devices: 210 us -> 197 us
  other arithmetic: 24.2 us -> 18.5 us
  starting transfers between devices: 16.2 us -> 20.6 us
    all_gather x1, waiting for transfers between devices: 52.7 us -> 10.6 us  [body(): lax.all_gather(select(keys_values, 2), ('tile', 'seq'), axis=0, tiled=True)]
    all_to_all x0 -> x1, waiting for transfers between devices: none -> 34 us  [gather_by_exchange(): return lax.all_to_all(copies, axis, dim, dim, tiled=True)]
    all_gather x1 -> x0, waiting for transfers between devices: 8.69 us -> none  [body(): segment_kv = lax.all_gather(keys_values, 'seq', axis=0, tiled=True)]
    unnamed x29 -> x48, local copies, waits for them, and re-layouts: 6.38 us -> 11.3 us
    slice x2 -> x1, local copies, waits for them, and re-layouts: 6.41 us -> 1.87 us  [body(): segment_kv[:, :hidden_width].reshape(-1, HEAD_COUNT, HEAD_WIDTH)]
    all_to_all x0 -> x1, starting transfers between devices: none -> 4.44 us  [gather_by_exchange(): return lax.all_to_all(copies, axis, dim, dim, tiled=True)]
    reduce_scatter x1, waiting for transfers between devices: 68.9 us -> 73.2 us  [body(): lax.psum_scatter(jnp.dot(hidden, w_down, preferred_element_type=jnp.float...]
  transfers between devices with their start and end apart: 6 -> 6, of which waited for: 6 -> 6; matrix products, arithmetic and copies ran while one was open for 13% -> 7% of each run, Pallas kernels for 0% -> 0%
where the time goes in v1:
time: 323 us; the launch traced here: 322 us
  waiting for transfers between devices  197 us (61%)
  local copies, waits for them, and re-layouts  38.8 us (12%)
  matrix products  34 us (11%)
  starting transfers between devices  20.6 us (6%)
  other arithmetic  18.5 us (6%)
  between operations  13.5 us (4%)
    reduce_scatter x1, waiting for transfers between devices, body(): lax.psum_scatter(jnp.dot(hidden, w_down, preferred_element_type=jnp.float...  73.2 us
    all_gather x1, waiting for transfers between devices, body(): shard_rows = lax.all_gather(normed, 'tile', axis=0, tiled=True)  64.7 us
    all_to_all x1, waiting for transfers between devices, gather_by_exchange(): return lax.all_to_all(copies, axis, dim, dim, tiled=True)  34 us
    dot_general x1, matrix products, body(): jnp.dot(hidden, w_down, preferred_element_type=jnp.float32)  14.6 us
    unnamed x48, local copies, waits for them, and re-layouts  11.3 us
    all_gather x1, waiting for transfers between devices, body(): lax.all_gather(select(keys_values, 2), ('tile', 'seq'), axis=0, tiled=True)  10.6 us
    all_to_all x1, waiting for transfers between devices, body(): lax.all_to_all(meta_table.reshape(devices, capacity, 3), ('tile', 'seq'),...  8.54 us
    all_to_all x1, starting transfers between devices, body(): lax.all_to_all(meta_table.reshape(devices, capacity, 3), ('tile', 'seq'),...  8.32 us
  transfers between devices with their start and end apart: 6, of which 6 were waited for; matrix products, arithmetic and copies ran while one was open for 7% of the time, Pallas kernels for 0%

profile of v1, /device:TPU:1, one launch (start us, length us, event | category | flops | bytes accessed | tf_op | source)
XLA Modules:
  0.0 322.2 jit_solution(10520869918505830723)
XLA Ops:
  9.1 2.0 fusion.33
  11.2 64.7 %all-gather.3.cloned.1.call-done = bf16[2048,1536]{1,0:T(8,128)(2,1)} async-done(((bf16[128,1536]{1,0:T(8,128)(2,1)}), bf16[2048,1536]{1,0:T(8,128)(2,1)}) %all-gather.3.cloned.1.call-update) | async-done | bytes 6291472 | tf_op jit(solution)/shard_map/all_gather | solution.py:69
  75.9 6.1 %fusion.71 = f32[2048,256]{1,0:T(8,128)} fusion(bf16[2048,1536]{1,0:T(8,128)(2,1)} %all-gather.3.cloned.1.call-done, bf16[1536,256]{1,0:T(8,128)(2,1)} %param.16), kind=kOutput, calls=%fused_computation.121 | convolution fusion | flops 1610612736 | bytes 9175040 | tf_op jit(solution)/shard_map/dot_general | solution.py:70
  82.0 14.6 %fusion.7 = f32[2048,1536]{1,0:T(8,128)} fusion(bf16[256,1536]{1,0:T(8,128)(2,1)} %param.18, bf16[2048,1536]{1,0:T(8,128)(2,1)} %all-gather.3.cloned.1.call-done, bf16[1536,256]{1,0:T(8,128)(2,1)} %param.17, f32[2048,256]{1,0:T(8,128)} %fusion.71), kind=kOutput, calls=%fused_computation.14 | convolution fusion | flops 3224371200 | bytes 22544384 | tf_op jit(solution)/shard_map/dot_general | solution.py:74
  98.2 1.8 scatter_custom_fusion
  100.0 8.3 %all-to-all-start = ((s32[128,2,3]{2,1,0:T(2,128)}), s32[128,2,3]{2,1,0:T(2,128)}, u32[]{:S(2)}, u32[]{:S(2)}) async-start(s32[128,2,3]{2,1,0:T(2,128)} %bitcast.80), calls=%async_computation | async-start | bytes 262144 | tf_op jit(solution)/shard_map/all_to_all | solution.py:103
  109.6 8.5 %all-to-all-done = s32[128,2,3]{2,1,0:T(2,128)} async-done(((s32[128,2,3]{2,1,0:T(2,128)}), s32[128,2,3]{2,1,0:T(2,128)}, u32[]{:S(2)}, u32[]{:S(2)}) %all-to-all-start) | async-done | bytes 3104 | tf_op jit(solution)/shard_map/all_to_all | solution.py:103
  119.1 73.2 %reduce-scatter.2.cloned.1.call-done = f32[128,1536]{1,0:T(8,128)} async-done(((f32[2048,1536]{1,0:T(8,128)}), f32[128,1536]{1,0:T(8,128)}) %reduce-scatter.2.cloned.1.call-update) | async-done | bytes 786448 | tf_op jit(solution)/shard_map/reduce_scatter | solution.py:73
  192.3 1.4 fusion.39
  193.7 1.5 multiply_reduce_fusion.1
  195.2 3.3 %convolution_convert_fusion.1 = bf16[128,768]{1,0:T(8,128)(2,1)} fusion(bf16[1536,768]{1,0:T(8,128)(2,1)} %param.21, f32[1536]{0:T(1024)} %param.20, f32[128]{0:T(128)S(1)} %add_rsqrt_fusion.1, f32[128]{0:T(128)S(1)} %broadcast_multiply_fusion.1, bf16[128,1536]{1,0:T(8,128)(2,1)} %param.14, f32[128,1536]{1,0:T(8,128)} %reduce-scatter.2.cloned.1.call-done, ...), kind=kOutput, calls=%fused_computation.25 | convolution fusion | flops 303464448 | bytes 3748864 | tf_op jit(solution)/shard_map/dot_general | solution.py:81
  198.5 2.3 scatter_custom_fusion.1
  200.7 1.9 reshape.196
  202.6 7.8 %all-to-all-start.1 = ((bf16[128,2,768]{2,1,0:T(2,128)(2,1)}), bf16[128,2,768]{2,1,0:T(2,128)(2,1)}, u32[]{:S(2)}, u32[]{:S(2)}) async-start(bf16[128,2,768]{2,1,0:T(2,128)(2,1)} %reshape.196), calls=%async_computation.2 | async-start | bytes 786432 | tf_op jit(solution)/shard_map/all_to_all | solution.py:96
  211.0 2.2 scatter_custom_fusion.3
  214.3 2.5 multiply_sine_fusion.1
  216.8 5.7 %all-to-all-done.1 = bf16[128,2,768]{2,1,0:T(2,128)(2,1)} async-done(((bf16[128,2,768]{2,1,0:T(2,128)(2,1)}), bf16[128,2,768]{2,1,0:T(2,128)(2,1)}, u32[]{:S(2)}, u32[]{:S(2)}) %all-to-all-start.1) | async-done | bytes 393248 | tf_op jit(solution)/shard_map/all_to_all | solution.py:96
  222.5 1.9 reshape.226
  224.3 2.7 scatter_custom_fusion.2
  230.2 1.7 copy-done.7
  233.9 4.4 %all-to-all-start.2 = ((bf16[8,128,1536]{2,1,0:T(8,128)(2,1)}), bf16[8,128,1536]{2,1,0:T(8,128)(2,1)S(1)}, u32[]{:S(2)}, u32[]{:S(2)}) async-start(bf16[8,128,1536]{2,1,0:T(8,128)(2,1)} %bitcast.76), calls=%async_computation.3 | async-start | bytes 6291456 | tf_op jit(solution)/shard_map/all_to_all | solution.py:13
  241.3 1.9 select_reduce_fusion.1
  243.2 34.0 %all-to-all-done.2 = bf16[8,128,1536]{2,1,0:T(8,128)(2,1)S(1)} async-done(((bf16[8,128,1536]{2,1,0:T(8,128)(2,1)}), bf16[8,128,1536]{2,1,0:T(8,128)(2,1)S(1)}, u32[]{:S(2)}, u32[]{:S(2)}) %all-to-all-start.2) | async-done | bytes 3145760 | tf_op jit(solution)/shard_map/all_to_all | solution.py:13
  277.2 1.9 fusion.68
  279.1 1.8 copy.95
  281.0 1.7 copy.96
  283.7 2.7 copy-done.3
  286.4 1.9 fusion.1
  288.3 10.6 %all-gather.5.cloned.1.call-done = bf16[1024,1536]{1,0:T(8,128)(2,1)} async-done(((bf16[8,1536]{1,0:T(8,128)(2,1)}), bf16[1024,1536]{1,0:T(8,128)(2,1)}) %all-gather.5.cloned.1.call-update) | async-done | bytes 3145744 | tf_op jit(solution)/shard_map/all_gather | solution.py:148
  298.9 3.2 fusion.67
  302.1 1.7 copy.83
  309.8 4.8 %fusion.26 = bf16[128,12,64]{0,2,1:T(8,128)(2,1)S(1)} fusion(bf16[1024,12,64]{0,2,1:T(8,128)(2,1)} %bitcast.78, f32[12,128,1024]{2,1,0:T(8,128)} %copy-done.3, f32[12,128]{1,0:T(8,128)S(1)} %get-tuple-element.25, f32[128,12,64]{0,2,1:T(8,128)} %copy.89, f32[128,12]{0,1:T(8,128)S(1)} %get-tuple-element.8, f32[128,12]{0,1:T(8,128)} %bitcast.83, ...), kind=kOutput, calls=%fused_computation.33 | convolution fusion | flops 206635008 | bytes 8480256 | tf_op jit(solution)/shard_map/hqk,khd->qhd/dot_general | solution.py:42
  (93 shorter events, 24.2 us)
Async XLA Ops:
  6.5 222.1 %copy-start = (bf16[768,2304]{1,0:T(8,128)(2,1)S(1)}, bf16[768,2304]{1,0:T(8,128)(2,1)}, u32[]{:S(2)}) copy-start(bf16[768,2304]{1,0:T(8,128)(2,1)} %param.25) | copy-start | bytes 10616836
  6.5 69.4 %all-gather.3.cloned.1.call-start = ((), (), s32[]{:S(2)}) async-start(), calls=%async_computation.4 | async-start | bytes 6684672 | tf_op jit(solution)/shard_map/all_gather | solution.py:69
  11.1 181.2 %reduce-scatter.2.cloned.1.call-start = ((), (), s32[]{:S(2)}) async-start(), calls=%async_computation.5 | async-start | bytes 13369344 | tf_op jit(solution)/shard_map/reduce_scatter | solution.py:73
  96.6 0.7 copy-start.15
  96.6 0.7 copy-start.17
  96.6 95.7 %copy-start.9 = (f32[1536]{0:T(1024)S(1)}, f32[1536]{0:T(1024)}, u32[]{:S(2)}) copy-start(f32[1536]{0:T(1024)} %param.19) | copy-start | bytes 18436
  98.2 1.8 copy-start.18
  100.0 18.1 %all-to-all-start = ((s32[128,2,3]{2,1,0:T(2,128)}), s32[128,2,3]{2,1,0:T(2,128)}, u32[]{:S(2)}, u32[]{:S(2)}) async-start(s32[128,2,3]{2,1,0:T(2,128)} %bitcast.80), calls=%async_computation | async-start | bytes 262144 | tf_op jit(solution)/shard_map/all_to_all | solution.py:103
  198.5 30.2 %copy-start.14 = (f32[768]{0:T(1024)S(1)}, f32[768]{0:T(1024)}, u32[]{:S(2)}) copy-start(f32[768]{0:T(1024)} %param.24) | copy-start | bytes 9220
  202.6 19.8 %all-to-all-start.1 = ((bf16[128,2,768]{2,1,0:T(2,128)(2,1)}), bf16[128,2,768]{2,1,0:T(2,128)(2,1)}, u32[]{:S(2)}, u32[]{:S(2)}) async-start(bf16[128,2,768]{2,1,0:T(2,128)(2,1)} %reshape.196), calls=%async_computation.2 | async-start | bytes 786432 | tf_op jit(solution)/shard_map/all_to_all | solution.py:96
  210.4 88.5 %all-gather.5.cloned.1.call-start = ((), (), s32[]{:S(2)}) async-start(), calls=%async_computation.6 | async-start | bytes 3170304 | tf_op jit(solution)/shard_map/all_gather | solution.py:148
  210.5 0.5 copy-start.16
  228.5 1.0 copy-start.5
  229.4 0.8 copy-start.2
  230.2 1.7 copy-start.7
  233.9 43.3 %all-to-all-start.2 = ((bf16[8,128,1536]{2,1,0:T(8,128)(2,1)}), bf16[8,128,1536]{2,1,0:T(8,128)(2,1)S(1)}, u32[]{:S(2)}, u32[]{:S(2)}) async-start(bf16[8,128,1536]{2,1,0:T(8,128)(2,1)} %bitcast.76), calls=%async_computation.3 | async-start | bytes 6291456 | tf_op jit(solution)/shard_map/all_to_all | solution.py:13
  279.1 1.9 copy-start.4
  283.7 2.7 copy-start.3
  305.2 0.6 copy-start.10
  307.3 2.4 copy-start.11
  307.3 2.4 copy-start.12
  307.3 2.4 copy-start.13
  309.7 4.9 %copy-start.6 = (f32[128,768]{1,0:T(8,128)S(1)}, f32[128,768]{1,0:T(8,128)}, u32[]{:S(2)}) copy-start(f32[128,768]{1,0:T(8,128)} %copy-done.5) | copy-start | bytes 1179652
  309.7 4.9 %copy-start.8 = (bf16[768,768]{1,0:T(8,128)(2,1)S(1)}, bf16[768,768]{1,0:T(8,128)(2,1)}, u32[]{:S(2)}) copy-start(bf16[768,768]{1,0:T(8,128)(2,1)} %param.27) | copy-start | bytes 3538948
  309.8 5.9 %copy-start.1 = (bf16[768,2304]{1,0:T(8,128)(2,1)S(1)}, bf16[768,2304]{1,0:T(8,128)(2,1)}, u32[]{:S(2)}) copy-start(bf16[768,2304]{1,0:T(8,128)(2,1)} %param.25) | copy-start | bytes 10616836
Sparse Core Ops, SparseCore 0:
  11.3 64.6 all-gather.2
  96.7 95.5 reduce-scatter.1
  234.0 64.8 all-gather.4
